TPU v7x, 128 devices: a whole 4x4x4 slice. The times are simulated.
128 devices in a mesh: role: 2 (over y_lo), grp: 16 (over x, z), tp: 4 (over y_hi, core).
Axes of the slice: x: 4, y: 4 (y_hi: 2, y_lo: 2; y = y_hi * 2 + y_lo), z: 4, core: 2. Of those that a mesh axis runs over, the one named last changes fastest.
Arguments:
- q_latent: bfloat16 [1024, 64, 576], P(('role', 'grp', 'tp')), may hold values from -60 to 60
- kv_new: bfloat16 [1024, 576], P(('role', 'grp', 'tp')), may hold values from -6 to 6
- kv_cache: bfloat16 [1024, 1024, 576], P(('role', 'grp', 'tp')), may hold values from -6 to 6
- lengths: int32 [1024], P(('role', 'grp', 'tp')), may hold values from 2 to 1024, as said below
- members: int32 [1024], P(('role', 'grp', 'tp')), may hold values from 0 to 7, as said below
- hidden_in: bfloat16 [1024, 7168], P('role', 'grp'), may hold values from -40 to 40
- w_uv: bfloat16 [64, 512, 128], P('tp'), may hold values from -1.5 to 1.5
- w_o: bfloat16 [8192, 7168], P('tp', 'grp'), may hold values from -0.0625 to 0.0625
- norm_gain: bfloat16 [7168], P('grp'), may hold values from 0.5 to 1.5
- w_gate: bfloat16 [7168, 18432], P('grp', ('role', 'tp')), may hold values from -0.09375 to 0.09375
- w_up: bfloat16 [7168, 18432], P('grp', ('role', 'tp')), may hold values from -0.0625 to 0.0625
- w_down: bfloat16 [18432, 7168], P(('role', 'tp'), 'grp'), may hold values from -0.046875 to 0.046875
Outputs:
- layer_out: bfloat16 [1024, 7168], P(('role', 'grp'))
Inputs may be any that keep to these rules, and one draw needn't show every extreme that they name: `lengths`: each request's cache is valid at positions 0 to its length - 1. Within each aligned block of 8 tokens, members is a permutation of 0 to 7.
All inputs are finite; a program needn't handle non-finite values.
Results may differ from a plain program's by a relative error of at most 0.017.
Values may be sent and summed in bfloat16 or wider, within the bound.
No kernel may reach another device: no remote copies, remote signals or barrier semaphores. Data moves between devices by JAX's collectives and lax.ppermute only.
A program may use at most 128 MiB of HBM per device.

v0:
```python
import jax
import jax.numpy as jnp
from jax import lax
from jax.sharding import PartitionSpec as P

epsilon = 1e-06


def body(
    q_latent,
    kv_new,
    kv_cache,
    lengths,
    members,
    hidden_in,
    w_uv,
    w_o,
    norm_gain,
    w_gate,
    w_up,
    w_down,
):
    groups = lax.axis_size("grp")
    splits = lax.axis_size("tp")
    per_batch = q_latent.shape[0] // 2
    latent = w_uv.shape[1]
    ctx_len = kv_cache.shape[1]
    width_dev = w_o.shape[1]
    model_width = width_dev * groups
    rows_role = groups * splits * per_batch
    score_scale = (w_uv.shape[2] + kv_cache.shape[2] - latent) ** (-0.5)
    positions = jnp.arange(ctx_len, dtype=jnp.int32)
    gain = norm_gain.astype(jnp.float32)
    residual_in = hidden_in.reshape(groups, splits, 2, per_batch, width_dev)
    outputs = []
    for micro_batch in range(2):
        first_row = micro_batch * per_batch
        chosen = members[first_row : first_row + per_batch]
        queries = q_latent[first_row : first_row + per_batch]
        newest = kv_new[first_row : first_row + per_batch]
        cache_rows = jnp.take(kv_cache, chosen, axis=0)
        cache_len = jnp.take(lengths, chosen)
        scores = (
            jnp.einsum("rhk,rpk->rhp", queries, cache_rows, preferred_element_type=jnp.float32)
            * score_scale
        )
        own_score = (
            jnp.einsum("rhk,rk->rh", queries, newest, preferred_element_type=jnp.float32)
            * score_scale
        )
        usable = positions[None, None, :] < cache_len[:, None, None]
        peak = jnp.maximum(jnp.max(jnp.where(usable, scores, -1e30), axis=2), own_score)
        probs = jnp.where(usable, jnp.exp(scores - peak[..., None]), 0.0).astype(jnp.bfloat16)
        self_weight = jnp.exp(own_score - peak)
        denom = jnp.sum(probs.astype(jnp.float32), axis=2) + self_weight
        accum = jnp.einsum(
            "rhp,rpl->rhl", probs, cache_rows[:, :, :latent], preferred_element_type=jnp.float32
        )
        accum = accum + self_weight[..., None] * newest[:, None, :latent].astype(jnp.float32)
        context = (accum / denom[..., None]).astype(jnp.bfloat16)
        spread = lax.all_to_all(context, "tp", split_axis=1, concat_axis=0, tiled=True)
        attend_values = jnp.einsum("thl,hlv->thv", spread, w_uv, preferred_element_type=jnp.float32)
        attn_part = jnp.dot(
            lax.all_gather(
                attend_values.astype(jnp.bfloat16).reshape(spread.shape[0], -1),
                "grp",
                axis=0,
                tiled=True,
            ),
            w_o,
            preferred_element_type=jnp.float32,
        )
        attn_out = lax.psum(attn_part, "tp")
        stream = (
            residual_in[:, :, micro_batch].reshape(rows_role, width_dev).astype(jnp.float32)
            + attn_out
        )
        square_sum = lax.psum(jnp.sum(stream * stream, axis=1), "grp")
        normed = (stream * lax.rsqrt(square_sum[:, None] / model_width + epsilon) * gain).astype(
            jnp.bfloat16
        )
        paired_rows = lax.all_gather(normed, "role", axis=0, tiled=True)
        gate_part = jnp.dot(paired_rows, w_gate, preferred_element_type=jnp.float32)
        up_part = jnp.dot(paired_rows, w_up, preferred_element_type=jnp.float32)
        gate_sum = lax.psum_scatter(gate_part, "grp", scatter_dimension=1, tiled=True)
        up_sum = lax.psum_scatter(up_part, "grp", scatter_dimension=1, tiled=True)
        share = (jax.nn.silu(gate_sum) * up_sum).astype(jnp.bfloat16)
        down_part = jnp.dot(
            lax.all_gather(share, "grp", axis=1, tiled=True),
            w_down,
            preferred_element_type=jnp.float32,
        )
        own_rows = lax.psum_scatter(down_part, "role", scatter_dimension=0, tiled=True)
        down_total = lax.psum(own_rows, "tp")
        result = (stream + down_total).astype(jnp.bfloat16)
        outputs.append(lax.all_to_all(result, "grp", split_axis=0, concat_axis=1, tiled=True))
    stacked = jnp.stack(outputs).reshape(2, splits, per_batch, model_width)
    return jnp.transpose(stacked, (1, 0, 2, 3)).reshape(splits * 2 * per_batch, model_width)


def solution(mesh):
    in_specs = (
        P(("role", "grp", "tp"), None, None),
        P(("role", "grp", "tp"), None),
        P(("role", "grp", "tp"), None, None),
        P(("role", "grp", "tp")),
        P(("role", "grp", "tp")),
        P("role", "grp"),
        P("tp", None, None),
        P("tp", "grp"),
        P("grp"),
        P("grp", ("role", "tp")),
        P("grp", ("role", "tp")),
        P(("role", "tp"), "grp"),
    )
    out_specs = P(("role", "grp"), None)
    return jax.shard_map(body, mesh=mesh, in_specs=in_specs, out_specs=out_specs, check_vma=False)
```

profile of v0, /device:TPU:1, one launch (start us, length us, event | category | flops | bytes accessed | tf_op | source)
XLA Modules:
  0.0 800.6 jit_solution(13518390291308960175)
XLA Ops:
  6.5 0.9 compare_and_fusion.1
  7.5 1.3 gather_fusion
  8.8 1.3 gather_fusion.2
  10.0 6.7 gather_fusion.1
  16.8 6.8 gather_fusion.3
  23.6 7.7 copy.51
  31.3 7.8 copy.59
  39.3 9.2 %broadcast_select_fusion = (bf16[4,1024,576]{2,1,0:T(8,128)(2,1)}, bf16[4,1024,576]{2,1,0:T(8,128)(2,1)}) fusion(bf16[4,1024,576]{2,1,0:T(8,128)(2,1)} %copy.59, pred[4]{0:T(512)(128)(4,1)S(1)} %get-tuple-element.33, bf16[4,1024,576]{2,1,0:T(8,128)(2,1)} %copy.51, pred[4]{0:T(512)(128)(4,1)S(1)} %get-tuple-element.19), kind=kLoop, calls=%fused_computation.4 | loop fusion | flops 4718592 | bytes 18874376 | tf_op jit(solution)/shard_map/jit(_take)/select_n | solution.py:41
  48.6 4.4 select_reduce_fusion.1
  53.0 0.4 convert_reduce_fusion.1
  53.4 0.9 fusion.21
  54.3 0.9 copy.53
  55.3 6.0 all-to-all-start
  61.4 6.5 all-to-all-done
  68.1 0.4 fusion.10
  68.5 0.6 copy.87
  69.3 4.5 select_reduce_fusion
  73.8 0.4 convert_reduce_fusion
  74.2 0.9 fusion.15
  75.3 9.8 %all_to_all.68 = bf16[4,64,512]{2,0,1:T(4,128)(2,1)S(1)} all-to-all(bf16[4,64,512]{2,0,1:T(4,128)(2,1)S(1)} %copy.61), channel_id=1, replica_groups=mesh['role'=2,'grp'=16,'tp'=4] {'tp'}, dimensions={1} | all-to-all | bytes 524288 | tf_op jit(solution)/shard_map/all_to_all | solution.py:61
  85.3 0.4 fusion.11
  85.7 0.6 copy.86
  86.4 24.4 %all-gather.5.cloned.1.call-done = bf16[256,2048]{1,0:T(8,128)(2,1)} async-done(((bf16[16,2048]{1,0:T(8,128)(2,1)}), bf16[256,2048]{1,0:T(8,128)(2,1)}) %all-gather.5.cloned.1.call-update) | async-done | bytes 1048592 | tf_op jit(solution)/shard_map/all_gather | solution.py:64
  110.7 3.3 fusion.34
  114.0 41.0 %all-gather.9.cloned.1.call-done = bf16[256,2048]{1,0:T(8,128)(2,1)} async-done(((bf16[16,2048]{1,0:T(8,128)(2,1)}), bf16[256,2048]{1,0:T(8,128)(2,1)}) %all-gather.9.cloned.1.call-update) | async-done | bytes 1048592 | tf_op jit(solution)/shard_map/all_gather | solution.py:64
  155.0 2.7 fusion.37
  158.1 0.3 slice_convert_fusion.1
  159.2 44.4 %all-reduce.8.cloned.1.call-done = (f32[256,448]{0,1:T(8,128)}, f32[256,448]{0,1:T(8,128)}) async-done(((f32[256,448]{0,1:T(8,128)}, f32[256,448]{0,1:T(8,128)}), (f32[256,448]{0,1:T(8,128)}, f32[256,448]{0,1:T(8,128)})) %all-reduce.8.cloned.1.call-update) | async-done | bytes 917520 | tf_op jit(solution)/shard_map/psum | solution.py:73
  203.6 1.1 multiply_reduce_fusion.1
  204.7 1.1 multiply_reduce_fusion
  205.8 33.3 %all-reduce = (f32[256]{0:T(256)S(1)}, f32[256]{0:T(256)S(1)}) all-reduce(f32[256]{0:T(256)S(1)} %get-tuple-element.15, f32[256]{0:T(256)S(1)} %get-tuple-element.13), channel_id=1, replica_groups=mesh['role'=2,'grp'=16,'tp'=4] {'grp'}, use_global_device_ids=true, to_apply=%region_13.16 | all-reduce | flops 512 | bytes 4096 | tf_op jit(solution)/shard_map/psum | solution.py:78
  239.1 0.8 multiply_convert_fusion.1
  240.0 6.0 all_gather.19
  246.0 3.7 fusion.35
  249.7 5.2 fusion.36
  255.0 5.8 all_gather.22
  260.7 3.6 fusion.38
  264.4 1.5 copy-done.3
  265.9 3.6 fusion.39
  269.6 59.4 %reduce-scatter.7.cloned.1.call-done = f32[512,144]{0,1:T(8,128)} async-done(((f32[512,2304]{0,1:T(8,128)}), f32[512,144]{0,1:T(8,128)}) %reduce-scatter.7.cloned.1.call-update) | async-done | bytes 294928 | tf_op jit(solution)/shard_map/reduce_scatter | solution.py:85
  329.0 80.9 %reduce-scatter.9.cloned.1.call-done = f32[512,144]{0,1:T(8,128)} async-done(((f32[512,2304]{0,1:T(8,128)}), f32[512,144]{0,1:T(8,128)}) %reduce-scatter.9.cloned.1.call-update) | async-done | bytes 294928 | tf_op jit(solution)/shard_map/reduce_scatter | solution.py:86
  409.9 1.8 multiply_convert_fusion.3
  411.7 79.0 %reduce-scatter.13.cloned.1.call-done = f32[512,144]{0,1:T(8,128)} async-done(((f32[512,2304]{0,1:T(8,128)}), f32[512,144]{0,1:T(8,128)}) %reduce-scatter.13.cloned.1.call-update) | async-done | bytes 294928 | tf_op jit(solution)/shard_map/reduce_scatter | solution.py:85
  490.8 81.3 %reduce-scatter.15.cloned.1.call-done = f32[512,144]{0,1:T(8,128)} async-done(((f32[512,2304]{0,1:T(8,128)}), f32[512,144]{0,1:T(8,128)}) %reduce-scatter.15.cloned.1.call-update) | async-done | bytes 294928 | tf_op jit(solution)/shard_map/reduce_scatter | solution.py:86
  572.0 1.8 multiply_convert_fusion.2
  573.9 46.0 %all-gather.7.cloned.1.call-done = bf16[512,2304]{0,1:T(8,128)(2,1)} async-done(((bf16[512,144]{0,1:T(8,128)(2,1)}), bf16[512,2304]{0,1:T(8,128)(2,1)}) %all-gather.7.cloned.1.call-update) | async-done | bytes 2359312 | tf_op jit(solution)/shard_map/all_gather | solution.py:89
  619.9 3.8 fusion.40
  623.8 43.4 %all-gather.11.cloned.1.call-done = bf16[512,2304]{0,1:T(8,128)(2,1)} async-done(((bf16[512,144]{0,1:T(8,128)(2,1)}), bf16[512,2304]{0,1:T(8,128)(2,1)}) %all-gather.11.cloned.1.call-update) | async-done | bytes 2359312 | tf_op jit(solution)/shard_map/all_gather | solution.py:89
  667.2 3.8 fusion.41
  671.1 20.0 %reduce-scatter.11.cloned.1.call-done = f32[256,448]{0,1:T(8,128)} async-done(((f32[512,448]{0,1:T(8,128)}), f32[256,448]{0,1:T(8,128)}) %reduce-scatter.11.cloned.1.call-update) | async-done | bytes 458768 | tf_op jit(solution)/shard_map/reduce_scatter | solution.py:93
  691.0 24.9 %reduce-scatter.17.cloned.1.call-done = f32[256,448]{0,1:T(8,128)} async-done(((f32[512,448]{0,1:T(8,128)}), f32[256,448]{0,1:T(8,128)}) %reduce-scatter.17.cloned.1.call-update) | async-done | bytes 458768 | tf_op jit(solution)/shard_map/reduce_scatter | solution.py:93
  715.9 48.4 %all-reduce.6.cloned.1.call-done = (f32[256,448]{0,1:T(8,128)}, f32[256,448]{0,1:T(8,128)}) async-done(((f32[256,448]{0,1:T(8,128)}, f32[256,448]{0,1:T(8,128)}), (f32[256,448]{0,1:T(8,128)}, f32[256,448]{0,1:T(8,128)})) %all-reduce.6.cloned.1.call-update) | async-done | bytes 917520 | tf_op jit(solution)/shard_map/psum | solution.py:94
  764.4 1.1 add_convert_fusion.1
  765.4 0.8 copy.57
  766.3 6.7 all-to-all-start.1
  772.9 1.1 add_convert_fusion
  774.0 0.8 copy.65
  774.8 5.9 all-to-all-done.1
  780.7 3.9 all-to-all-start.3
  784.7 0.3 stack.9
  785.1 6.8 all-to-all-done.3
  792.1 0.3 stack.10
  792.4 0.3 maximum_bitcast_fusion
  792.9 0.9 reshape.103
  (80 shorter events, 3.4 us)
Async XLA Ops:
  6.5 61.6 %copy-start = (bf16[16,512,128]{2,1,0:T(8,128)(2,1)S(1)}, bf16[16,512,128]{2,1,0:T(8,128)(2,1)}, u32[]{:S(2)}) copy-start(bf16[16,512,128]{2,1,0:T(8,128)(2,1)} %param.22) | copy-start | bytes 6291460
  16.8 6.8 copy-start.8
  31.3 7.8 copy-start.6
  48.6 4.8 copy-start.5
  55.3 12.6 %all-to-all-start = ((bf16[4,64,512]{2,0,1:T(4,128)(2,1)}), bf16[4,64,512]{2,0,1:T(4,128)(2,1)S(1)}, u32[]{:S(2)}, u32[]{:S(2)}) async-start(bf16[4,64,512]{2,0,1:T(4,128)(2,1)} %copy.53), calls=%async_computation | async-start | bytes 524288 | tf_op jit(solution)/shard_map/all_to_all | solution.py:61
  61.2 49.5 %all-gather.5.cloned.1.call-start = ((), (), s32[]{:S(2)}) async-start(), calls=%async_computation.10 | async-start | bytes 1114112 | tf_op jit(solution)/shard_map/all_gather | solution.py:64
  68.1 6.0 slice-start
  69.1 85.9 %all-gather.9.cloned.1.call-start = ((), (), s32[]{:S(2)}) async-start(), calls=%async_computation.15 | async-start | bytes 1114112 | tf_op jit(solution)/shard_map/all_gather | solution.py:64
  69.3 4.9 slice-start.1
  85.7 69.4 %copy-start.4 = (bf16[2048,448]{0,1:T(8,128)(2,1)S(1)}, bf16[2048,448]{0,1:T(8,128)(2,1)}, u32[]{:S(2)}) copy-start(bf16[2048,448]{0,1:T(8,128)(2,1)} %param.23) | copy-start | bytes 5505028
  86.3 117.3 %all-reduce.8.cloned.1.call-start = ((), (), s32[]{:S(2)}) async-start(), calls=%async_computation.21 | async-start | bytes 1835008 | tf_op jit(solution)/shard_map/psum | solution.py:73
  114.0 43.7 %copy-start.7 = (bf16[512,448]{0,1:T(8,128)(2,1)S(1)}, bf16[512,448]{0,1:T(8,128)(2,1)}, u32[]{:S(2)}) copy-start(bf16[512,448]{0,1:T(8,128)(2,1)} %param.21) | copy-start | bytes 1376260
  157.7 171.2 %reduce-scatter.7.cloned.1.call-start = ((), (), s32[]{:S(2)}) async-start(), calls=%async_computation.11 | async-start | bytes 5013504 | tf_op jit(solution)/shard_map/reduce_scatter | solution.py:85
  158.1 1.1 copy-start.9
  159.2 86.8 %copy-start.2 = (bf16[448,2304]{1,0:T(8,128)(2,1)S(1)}, bf16[448,2304]{1,0:T(8,128)(2,1)}, u32[]{:S(2)}) copy-start(bf16[448,2304]{1,0:T(8,128)(2,1)} %param.25) | copy-start | bytes 6193156
  249.7 160.2 %reduce-scatter.9.cloned.1.call-start = ((), (), s32[]{:S(2)}) async-start(), calls=%async_computation.12 | async-start | bytes 5013504 | tf_op jit(solution)/shard_map/reduce_scatter | solution.py:86
  254.9 235.8 %reduce-scatter.13.cloned.1.call-start = ((), (), s32[]{:S(2)}) async-start(), calls=%async_computation.16 | async-start | bytes 5013504 | tf_op jit(solution)/shard_map/reduce_scatter | solution.py:85
  264.3 1.6 copy-start.3
  264.4 307.7 %reduce-scatter.15.cloned.1.call-start = ((), (), s32[]{:S(2)}) async-start(), calls=%async_computation.17 | async-start | bytes 5013504 | tf_op jit(solution)/shard_map/reduce_scatter | solution.py:86
  269.5 350.4 %copy-start.10 = (bf16[2304,448]{0,1:T(8,128)(2,1)S(1)}, bf16[2304,448]{0,1:T(8,128)(2,1)}, u32[]{:S(2)}) copy-start(bf16[2304,448]{0,1:T(8,128)(2,1)} %param.27) | copy-start | bytes 6193156
  269.6 350.3 %all-gather.7.cloned.1.call-start = ((), (), s32[]{:S(2)}) async-start(), calls=%async_computation.13 | async-start | bytes 2506752 | tf_op jit(solution)/shard_map/all_gather | solution.py:89
  411.7 255.5 %all-gather.11.cloned.1.call-start = ((), (), s32[]{:S(2)}) async-start(), calls=%async_computation.18 | async-start | bytes 2506752 | tf_op jit(solution)/shard_map/all_gather | solution.py:89
  573.8 117.2 %reduce-scatter.11.cloned.1.call-start = ((), (), s32[]{:S(2)}) async-start(), calls=%async_computation.14 | async-start | bytes 1376256 | tf_op jit(solution)/shard_map/reduce_scatter | solution.py:93
  623.7 92.1 %reduce-scatter.17.cloned.1.call-start = ((), (), s32[]{:S(2)}) async-start(), calls=%async_computation.19 | async-start | bytes 1376256 | tf_op jit(solution)/shard_map/reduce_scatter | solution.py:93
  671.0 93.3 %all-reduce.6.cloned.1.call-start = ((), (), s32[]{:S(2)}) async-start(), calls=%async_computation.20 | async-start | bytes 1835008 | tf_op jit(solution)/shard_map/psum | solution.py:94
  766.3 14.5 %all-to-all-start.1 = ((bf16[16,16,448]{2,1,0:T(8,128)(2,1)}), bf16[16,16,448]{2,1,0:T(8,128)(2,1)S(1)}, u32[]{:S(2)}, u32[]{:S(2)}) async-start(bf16[16,16,448]{2,1,0:T(8,128)(2,1)} %bitcast.6), calls=%async_computation.4 | async-start | bytes 524288 | tf_op jit(solution)/shard_map/all_to_all | solution.py:96
  780.7 13.1 %copy-start.1 = (bf16[16,512,128]{2,1,0:T(8,128)(2,1)S(1)}, bf16[16,512,128]{2,1,0:T(8,128)(2,1)}, u32[]{:S(2)}) copy-start(bf16[16,512,128]{2,1,0:T(8,128)(2,1)} %param.22) | copy-start | bytes 6291460
  780.7 11.2 %all-to-all-start.3 = ((bf16[16,16,448]{2,1,0:T(8,128)(2,1)}), bf16[16,16,448]{2,1,0:T(8,128)(2,1)S(1)}, u32[]{:S(2)}, u32[]{:S(2)}) async-start(bf16[16,16,448]{2,1,0:T(8,128)(2,1)} %bitcast.14), calls=%async_computation.9 | async-start | bytes 524288 | tf_op jit(solution)/shard_map/all_to_all | solution.py:96
Sparse Core Ops, SparseCore 0:
  69.3 41.4 all-gather.4
  112.9 42.0 all-gather.8
  157.8 45.7 all-reduce.7
  249.8 79.0 reduce-scatter.6
  332.1 77.6 reduce-scatter.8
  413.1 77.6 reduce-scatter.12
  494.1 77.8 reduce-scatter.14
  574.2 45.6 all-gather.6
  622.1 45.0 all-gather.10
  669.4 21.6 reduce-scatter.10
  693.5 22.3 reduce-scatter.16
  718.3 45.9 all-reduce.5
where the time goes:
time: 803 us; the launch traced here: 801 us
  waiting for transfers between devices  612 us (76%)
  blocking collectives  54.8 us (7%)
  matrix products  41.6 us (5%)
  local copies, waits for them, and re-layouts  40.7 us (5%)
  other arithmetic  20.5 us (3%)
  starting transfers between devices  16.9 us (2%)
  between operations  13.9 us (2%)
    reduce_scatter x2, waiting for transfers between devices, body(): up_sum = lax.psum_scatter(up_part, 'grp', scatter_dimension=1, tiled=True)  162 us
    reduce_scatter x2, waiting for transfers between devices, body(): lax.psum_scatter(gate_part, 'grp', scatter_dimension=1, tiled=True)  138 us
    all_gather x2, waiting for transfers between devices, body(): lax.all_gather(share, 'grp', axis=1, tiled=True)  89.4 us
    all_gather x2, waiting for transfers between devices, body(): lax.all_gather(attend_values.astype(jnp.bfloat16).reshape(spread.shape[0]...  65.3 us
    psum x1, waiting for transfers between devices, body(): down_total = lax.psum(own_rows, 'tp')  48.4 us
    reduce_scatter x2, waiting for transfers between devices, body(): lax.psum_scatter(down_part, 'role', scatter_dimension=0, tiled=True)  44.8 us
    psum x1, waiting for transfers between devices, body(): attn_out = lax.psum(attn_part, 'tp')  44.4 us
    psum x1, blocking collectives, body(): square_sum = lax.psum(jnp.sum(stream * stream, axis=1), 'grp')  33.3 us
  transfers between devices with their start and end apart: 15, of which 15 were waited for; matrix products, arithmetic and copies ran while one was open for 5% of the time, Pallas kernels for 0%

commit v1 on v0

v1 whole, which is shorter than its diff:
```python
import functools

import jax
import jax.numpy as jnp
from jax import lax
from jax.experimental import pallas as pl
from jax.experimental.pallas import tpu as pltpu
from jax.sharding import PartitionSpec as P

epsilon = 1e-06
VMEM_LIMIT = 48 * 1024 * 1024


def attend_kernel(scale, latent, members_ref, lengths_ref, q_ref, new_ref, kv_ref, out_ref):
    token = pl.program_id(0)
    length = lengths_ref[members_ref[token]]
    queries = q_ref[0]
    cache = kv_ref[0]
    newest = new_ref[0]
    scores = scale * lax.dot_general(
        queries, cache, (((1,), (1,)), ((), ())), preferred_element_type=jnp.float32
    )
    own = scale * jnp.sum(queries.astype(jnp.float32) * newest, axis=1, keepdims=True)
    usable = lax.broadcasted_iota(jnp.int32, scores.shape, 1) < length
    scores = jnp.where(usable, scores, -1e30)
    peak = jnp.maximum(jnp.max(scores, axis=1, keepdims=True), own)
    probs = jnp.exp(scores - peak).astype(jnp.bfloat16)
    self_weight = jnp.exp(own - peak)
    denom = jnp.sum(probs.astype(jnp.float32), axis=1, keepdims=True) + self_weight
    accum = jnp.dot(probs, cache[:, :latent], preferred_element_type=jnp.float32)
    accum = accum + self_weight * newest[:, :latent]
    out_ref[0] = (accum / denom).astype(out_ref.dtype)


def attend(q_latent, kv_new, kv_cache, lengths, members, scale, latent):
    tokens, heads, kv = q_latent.shape
    ctx = kv_cache.shape[1]
    grid_spec = pltpu.PrefetchScalarGridSpec(
        num_scalar_prefetch=2,
        grid=(tokens,),
        in_specs=[
            pl.BlockSpec((1, heads, kv), lambda t, m, n: (t, 0, 0)),
            pl.BlockSpec((1, 1, kv), lambda t, m, n: (t, 0, 0)),
            pl.BlockSpec((1, ctx, kv), lambda t, m, n: (m[t], 0, 0)),
        ],
        out_specs=pl.BlockSpec((1, heads, latent), lambda t, m, n: (t, 0, 0)),
    )
    return pl.pallas_call(
        functools.partial(attend_kernel, scale, latent),
        grid_spec=grid_spec,
        out_shape=jax.ShapeDtypeStruct((tokens, heads, latent), jnp.bfloat16),
        compiler_params=pltpu.CompilerParams(vmem_limit_bytes=VMEM_LIMIT),
        name="attend",
    )(members, lengths, q_latent, kv_new.astype(jnp.float32)[:, None, :], kv_cache)


def gate_up_kernel(x_ref, gain_ref, gate_ref, up_ref, out_ref):
    hidden = gate_ref.shape[1]
    x = x_ref[...].astype(jnp.float32)
    square = jnp.sum(x * x, axis=1, keepdims=True)
    scaled = (x * gain_ref[...]).astype(jnp.bfloat16)
    out_ref[:, :hidden] = jnp.dot(
        scaled, gate_ref[...], preferred_element_type=jnp.float32
    ).astype(jnp.bfloat16)
    out_ref[:, hidden : 2 * hidden] = jnp.dot(
        scaled, up_ref[...], preferred_element_type=jnp.float32
    ).astype(jnp.bfloat16)
    high = square.astype(jnp.bfloat16).astype(jnp.float32)
    lane = lax.broadcasted_iota(jnp.int32, (x.shape[0], 128), 1)
    out_ref[:, 2 * hidden :] = jnp.where(lane < 64, high, square - high).astype(jnp.bfloat16)


def gate_up(rows, gain, w_gate, w_up):
    count, width = rows.shape
    hidden = w_gate.shape[1]
    block = 256
    return pl.pallas_call(
        gate_up_kernel,
        grid=(count // block,),
        in_specs=[
            pl.BlockSpec((block, width), lambda i: (i, 0)),
            pl.BlockSpec((1, width), lambda i: (0, 0)),
            pl.BlockSpec((width, hidden), lambda i: (0, 0)),
            pl.BlockSpec((width, hidden), lambda i: (0, 0)),
        ],
        out_specs=pl.BlockSpec((block, 2 * hidden + 128), lambda i: (i, 0)),
        out_shape=jax.ShapeDtypeStruct((count, 2 * hidden + 128), jnp.bfloat16),
        compiler_params=pltpu.CompilerParams(vmem_limit_bytes=VMEM_LIMIT),
        name="gate_up",
    )(rows, gain, w_gate, w_up)


def spread_to(block, axis):
    size = lax.axis_size(axis)
    copies = jnp.broadcast_to(block[None], (size,) + block.shape)
    copies = lax.optimization_barrier(copies)
    landed = lax.all_to_all(copies, axis, split_axis=0, concat_axis=0)
    return landed.reshape((size * block.shape[0],) + block.shape[1:])


def body(
    q_latent,
    kv_new,
    kv_cache,
    lengths,
    members,
    hidden_in,
    w_uv,
    w_o,
    norm_gain,
    w_gate,
    w_up,
    w_down,
):
    groups = lax.axis_size("grp")
    splits = lax.axis_size("tp")
    roles = lax.axis_size("role")
    tokens, heads, kv = q_latent.shape
    latent = w_uv.shape[1]
    value_width = w_uv.shape[2]
    width_dev = w_o.shape[1]
    model_width = width_dev * groups
    hidden = w_gate.shape[1]
    score_scale = (value_width + kv - latent) ** (-0.5)

    context = attend(q_latent, kv_new, kv_cache, lengths, members, score_scale, latent)
    spread = lax.all_to_all(context, "tp", split_axis=1, concat_axis=0, tiled=True)
    values = jnp.einsum("thl,hlv->thv", spread, w_uv, preferred_element_type=jnp.float32)
    values = values.astype(jnp.bfloat16).reshape(spread.shape[0], -1)
    attn_part = jnp.dot(spread_to(values, "grp"), w_o, preferred_element_type=jnp.float32)
    attn_part = attn_part.astype(jnp.bfloat16).reshape(groups, splits, tokens, width_dev)
    landed = lax.all_to_all(attn_part, "tp", split_axis=1, concat_axis=1, tiled=True)
    attn_out = jnp.sum(landed.astype(jnp.float32), axis=1)
    residual = lax.dynamic_index_in_dim(
        hidden_in.reshape(groups, splits, tokens, width_dev),
        lax.axis_index("tp"),
        axis=1,
        keepdims=False,
    )
    stream = (residual.astype(jnp.float32) + attn_out).reshape(groups * tokens, width_dev)

    rows = spread_to(stream.astype(jnp.bfloat16), ("role", "tp"))
    parts = gate_up(rows, norm_gain.astype(jnp.float32)[None], w_gate, w_up)
    per_group = rows.shape[0] // groups
    landed = lax.all_to_all(
        parts.reshape(groups, per_group, -1), "grp", split_axis=0, concat_axis=0
    )
    sums = jnp.sum(landed.astype(jnp.float32), axis=0)
    square = sums[:, 2 * hidden : 2 * hidden + 1] + sums[:, 2 * hidden + 64 : 2 * hidden + 65]
    scale = lax.rsqrt(square / model_width + epsilon)
    activated = (
        jax.nn.silu(sums[:, :hidden] * scale) * (sums[:, hidden : 2 * hidden] * scale)
    ).astype(jnp.bfloat16)

    down_part = jnp.dot(spread_to(activated, "grp"), w_down, preferred_element_type=jnp.float32)
    down_part = down_part.astype(jnp.bfloat16).reshape(
        roles * splits, groups * tokens, width_dev
    )
    landed = lax.all_to_all(down_part, ("role", "tp"), split_axis=0, concat_axis=0)
    down = jnp.sum(landed.astype(jnp.float32), axis=0)
    result = (stream + down).astype(jnp.bfloat16).reshape(groups, tokens, width_dev)
    whole = lax.all_to_all(result, "grp", split_axis=0, concat_axis=2, tiled=True)
    return spread_to(whole.reshape(tokens, model_width), "tp")


def solution(mesh):
    in_specs = (
        P(("role", "grp", "tp"), None, None),
        P(("role", "grp", "tp"), None),
        P(("role", "grp", "tp"), None, None),
        P(("role", "grp", "tp")),
        P(("role", "grp", "tp")),
        P("role", "grp"),
        P("tp", None, None),
        P("tp", "grp"),
        P("grp"),
        P("grp", ("role", "tp")),
        P("grp", ("role", "tp")),
        P(("role", "tp"), "grp"),
    )
    out_specs = P(("role", "grp"), None)
    return jax.shard_map(body, mesh=mesh, in_specs=in_specs, out_specs=out_specs, check_vma=False)
```

time: 803 us -> 349 us (0.43)
  waiting for transfers between devices: 612 us -> 21.6 us
  blocking collectives: 54.8 us -> 267 us
  matrix products: 41.6 us -> 3.89 us
  local copies, waits for them, and re-layouts: 40.7 us -> 22.9 us
  Pallas kernels: 0 us -> 17.6 us
  other arithmetic: 20.5 us -> 3.13 us
  between operations: 13.9 us -> 0.25 us
    reduce_scatter x6 -> x0, waiting for transfers between devices: 345 us -> none  [the longest x2 162 us: body(): up_sum = lax.psum_scatter(up_part, 'grp', scatter_dimension=1, tiled=True)]
    all_to_all x0 -> x6, blocking collectives: none -> 252 us  [the longest x3 112 us: spread_to(): landed = lax.all_to_all(copies, axis, split_axis=0, concat_axis=0)]
    all_gather x4 -> x0, waiting for transfers between devices: 155 us -> none  [the longest x2 89.4 us: body(): lax.all_gather(share, 'grp', axis=1, tiled=True)]
    psum x2 -> x0, waiting for transfers between devices: 92.8 us -> none  [the longest x1 48.4 us: body(): down_total = lax.psum(own_rows, 'tp')]
    dot_general x14 -> x2, matrix products: 40.8 us -> 3.46 us  [the longest x1 2.32 us: body(): jnp.dot(spread_to(activated, 'grp'), w_down, preferred_element_type=jnp.f...]
    psum x1 -> x0, blocking collectives: 33.3 us -> none  [body(): square_sum = lax.psum(jnp.sum(stream * stream, axis=1), 'grp')]
    gather x6 -> x0, local copies, waits for them, and re-layouts: 31.6 us -> none  [the longest x4 29 us: body(): cache_rows = jnp.take(kv_cache, chosen, axis=0)]
    pallas_call x0 -> x2, Pallas kernels: none -> 17.6 us  [the longest x1 10.5 us: attend(): pl.pallas_call(functools.partial(attend_kernel, scale, latent), grid_spec...]
  transfers between devices with their start and end apart: 15 -> 2, of which waited for: 15 -> 2; matrix products, arithmetic and copies ran while one was open for 5% -> 0% of each run, Pallas kernels for 0% -> 0%
where the time goes in v1:
time: 349 us; the launch traced here: 348 us
  blocking collectives  267 us (77%)
  local copies, waits for them, and re-layouts  22.9 us (7%)
  waiting for transfers between devices  21.6 us (6%)
  Pallas kernels  17.6 us (5%)
  starting transfers between devices  12 us (3%)
  matrix products  3.89 us (1%)
    all_to_all x3, blocking collectives, spread_to(): landed = lax.all_to_all(copies, axis, split_axis=0, concat_axis=0)  112 us
    all_to_all x1, blocking collectives, body(): lax.all_to_all(parts.reshape(groups, per_group, -1), 'grp', split_axis=0,...  111 us
    all_to_all x1, blocking collectives, body(): lax.all_to_all(down_part, ('role', 'tp'), split_axis=0, concat_axis=0)  19.1 us
    unnamed x27, local copies, waits for them, and re-layouts  16.8 us
    all_to_all x1, blocking collectives, body(): lax.all_to_all(context, 'tp', split_axis=1, concat_axis=0, tiled=True)  15.1 us
    all_to_all x1, waiting for transfers between devices, spread_to(): landed = lax.all_to_all(copies, axis, split_axis=0, concat_axis=0)  12.3 us
    pallas_call x1, Pallas kernels, attend(): pl.pallas_call(functools.partial(attend_kernel, scale, latent), grid_spec...  10.5 us
    all_to_all x1, blocking collectives, body(): lax.all_to_all(result, 'grp', split_axis=0, concat_axis=2, tiled=True)  9.66 us
  transfers between devices with their start and end apart: 2, of which 2 were waited for; matrix products, arithmetic and copies ran while one was open for 0% of the time, Pallas kernels for 0%

profile of v1, /device:TPU:1, one launch (start us, length us, event | category | flops | bytes accessed | tf_op | source)
XLA Modules:
  0.0 348.0 jit_solution(376342045879081197)
XLA Ops:
  0.0 0.0 copy-start
  0.0 0.9 reshape.57.new_ref
  0.9 0.0 copy-start.4
  0.9 0.0 copy-start.5
  0.9 0.0 copy-start.6
  0.9 14.2 %copy.39.kv_ref = bf16[8,1024,576]{2,1,0:T(8,128)(2,1)} copy(bf16[8,1024,576]{1,2,0:T(8,128)(2,1)} %param.14) | data formatting | bytes 18874368 | tf_op args[2]
  15.1 0.0 copy-done.4
  15.1 0.0 copy-done.5
  15.1 0.0 copy-done.6
  15.1 10.5 %attend.1 = bf16[8,64,512]{2,1,0:T(8,128)(2,1)S(1)} custom-call(s32[8]{0:T(128)S(1)} %copy-done.5, s32[8]{0:T(128)S(1)} %copy-done.6, bf16[8,64,576]{2,1,0:T(8,128)(2,1)S(1)} %copy-done.4, f32[8,1,576]{2,1,0:T(1,128)S(1)} %reshape.57.new_ref, bf16[8,1024,576]{2,1,0:T(8,128)(2,1)} %copy.39.kv_ref), custom_call_target="tpu_custom_call" | custom-call | tf_op jit(solution)/shard_map/attend/pallas_call | solution.py:48
  25.6 0.3 copy.40
  25.9 15.1 %all_to_all.68 = bf16[8,64,512]{2,0,1:T(8,128)(2,1)S(1)} all-to-all(bf16[8,64,512]{2,0,1:T(8,128)(2,1)S(1)} %copy.40), channel_id=1, replica_groups=mesh['role'=2,'grp'=16,'tp'=4] {'tp'}, dimensions={1} | all-to-all | bytes 1048576 | tf_op jit(solution)/shard_map/all_to_all | solution.py:127
  41.0 0.0 copy-done
  41.0 0.4 fusion.1
  41.5 0.2 broadcast_in_dim.39
  41.7 0.0 copy-start.11
  41.7 33.4 %all_to_all.69 = bf16[16,32,2048]{2,1,0:T(8,128)(2,1)S(1)} all-to-all(bf16[16,32,2048]{2,1,0:T(8,128)(2,1)S(1)} %broadcast_in_dim.39), channel_id=1, replica_groups=mesh['role'=2,'grp'=16,'tp'=4] {'grp'}, dimensions={0} | all-to-all | bytes 4194304 | tf_op jit(solution)/shard_map/all_to_all | solution.py:97
  75.1 0.0 copy-done.11
  75.1 1.1 convolution_convert_fusion.1
  76.3 0.0 copy-start.8
  76.3 0.2 copy.43
  76.5 0.8 copy.44
  77.4 6.9 %all-to-all-start.2 = ((bf16[16,4,8,448]{3,2,0,1:T(8,128)(2,1)}), bf16[16,4,8,448]{3,2,0,1:T(8,128)(2,1)S(1)}, u32[]{:S(2)}, u32[]{:S(2)}) async-start(bf16[16,4,8,448]{3,2,0,1:T(8,128)(2,1)} %copy.44), calls=%async_computation.2 | async-start | bytes 1048576 | tf_op jit(solution)/shard_map/all_to_all | solution.py:132
  84.2 0.0 copy-done.8
  84.2 0.2 copy.38
  84.4 0.0 copy-start.7
  84.4 0.0 copy-start.9
  84.5 9.2 %all-to-all-done.2 = bf16[16,4,8,448]{3,2,0,1:T(8,128)(2,1)S(1)} async-done(((bf16[16,4,8,448]{3,2,0,1:T(8,128)(2,1)}), bf16[16,4,8,448]{3,2,0,1:T(8,128)(2,1)S(1)}, u32[]{:S(2)}, u32[]{:S(2)}) %all-to-all-start.2) | async-done | bytes 458784 | tf_op jit(solution)/shard_map/all_to_all | solution.py:132
  93.7 0.1 convert_reduce_fusion.2
  93.8 0.1 copy.45
  94.0 1.1 broadcast_in_dim.40
  95.1 0.0 copy-start.2
  95.1 0.0 copy-done.7
  95.1 5.1 %all-to-all-start.3 = ((bf16[8,128,448]{1,2,0:T(8,128)(2,1)}), bf16[8,128,448]{1,2,0:T(8,128)(2,1)}, u32[]{:S(2)}, u32[]{:S(2)}) async-start(bf16[8,128,448]{1,2,0:T(8,128)(2,1)} %broadcast_in_dim.40), calls=%async_computation.3 | async-start | bytes 1835008 | tf_op jit(solution)/shard_map/all_to_all | solution.py:97
  100.2 0.0 copy-done.9
  100.2 12.3 %all-to-all-done.3 = bf16[8,128,448]{1,2,0:T(8,128)(2,1)} async-done(((bf16[8,128,448]{1,2,0:T(8,128)(2,1)}), bf16[8,128,448]{1,2,0:T(8,128)(2,1)}, u32[]{:S(2)}, u32[]{:S(2)}) %all-to-all-start.3) | async-done | bytes 917536 | tf_op jit(solution)/shard_map/all_to_all | solution.py:97
  112.5 1.5 copy.46
  113.9 0.0 copy-done.2
  113.9 0.0 copy-start.3
  114.0 1.6 copy-done.3
  115.5 7.1 %gate_up.1 = bf16[1024,4736]{1,0:T(8,128)(2,1)} custom-call(bf16[1024,448]{1,0:T(8,128)(2,1)S(1)} %bitcast.53, f32[1,448]{1,0:T(1,128)S(1)} %bitcast.54, bf16[448,2304]{1,0:T(8,128)(2,1)S(1)} %copy-done.2, bf16[448,2304]{1,0:T(8,128)(2,1)S(1)} %copy-done.3), custom_call_target="tpu_custom_call" | custom-call | tf_op jit(solution)/shard_map/gate_up/pallas_call | solution.py:77
  122.7 111.1 %all_to_all.70 = bf16[16,64,4736]{2,1,0:T(8,128)(2,1)S(1)} all-to-all(bf16[16,64,4736]{2,1,0:T(8,128)(2,1)} %bitcast.55), channel_id=1, replica_groups=mesh['role'=2,'grp'=16,'tp'=4] {'grp'}, dimensions={0} | all-to-all | bytes 19398656 | tf_op jit(solution)/shard_map/all_to_all | solution.py:145
  233.8 1.4 convert_reduce_fusion
  235.2 0.2 fusion.14
  235.4 0.3 fusion.3
  235.6 0.4 broadcast_in_dim.43
  236.1 0.0 copy-start.10
  236.1 64.4 %all_to_all.71 = bf16[16,64,2304]{2,1,0:T(8,128)(2,1)S(1)} all-to-all(bf16[16,64,2304]{2,1,0:T(8,128)(2,1)S(1)} %broadcast_in_dim.43), channel_id=1, replica_groups=mesh['role'=2,'grp'=16,'tp'=4] {'grp'}, dimensions={0} | all-to-all | bytes 9437184 | tf_op jit(solution)/shard_map/all_to_all | solution.py:97
  300.5 0.0 copy-done.10
  300.5 2.3 fusion
  302.8 0.2 copy.60
  303.0 19.1 %all_to_all.72 = bf16[8,128,448]{1,2,0:T(8,128)(2,1)S(1)} all-to-all(bf16[8,128,448]{1,2,0:T(8,128)(2,1)S(1)} %bitcast.57), channel_id=1, replica_groups=mesh['role'=2,'grp'=16,'tp'=4] {'role','tp'}, dimensions={0} | all-to-all | bytes 1835008 | tf_op jit(solution)/shard_map/all_to_all | solution.py:159
  322.1 0.1 convert_reduce_fusion.1
  322.2 0.0 copy-start.1
  322.2 0.1 copy.49
  322.4 1.1 fusion.8
  323.5 9.7 %all_to_all.73 = bf16[16,8,448]{2,1,0:T(8,128)(2,1)S(1)} all-to-all(bf16[16,8,448]{2,1,0:T(8,128)(2,1)S(1)} %fusion.8), channel_id=1, replica_groups=mesh['role'=2,'grp'=16,'tp'=4] {'grp'}, dimensions={0} | all-to-all | bytes 229376 | tf_op jit(solution)/shard_map/all_to_all | solution.py:162
  333.2 0.2 broadcast_in_dim.44
  333.4 13.8 %all_to_all.74 = bf16[4,8,7168]{2,1,0:T(8,128)(2,1)S(1)} all-to-all(bf16[4,8,7168]{2,1,0:T(8,128)(2,1)S(1)} %broadcast_in_dim.45), channel_id=1, replica_groups=mesh['role'=2,'grp'=16,'tp'=4] {'tp'}, dimensions={0} | all-to-all | bytes 917504 | tf_op jit(solution)/shard_map/all_to_all | solution.py:97
  347.2 0.8 copy.63
  348.0 0.0 copy-done.1
  (5 shorter events, 0.1 us)
Async XLA Ops:
  0.0 41.0 %copy-start = (bf16[16,512,128]{2,1,0:T(8,128)(2,1)S(1)}, bf16[16,512,128]{2,1,0:T(8,128)(2,1)}, u32[]{:S(2)}) copy-start(bf16[16,512,128]{2,1,0:T(8,128)(2,1)} %param.18) | copy-start | bytes 6291460
  0.9 14.2 %copy-start.4 = (bf16[8,64,576]{2,1,0:T(8,128)(2,1)S(1)}, bf16[8,64,576]{2,1,0:T(8,128)(2,1)}, u32[]{:S(2)}) copy-start(bf16[8,64,576]{2,1,0:T(8,128)(2,1)} %q_ref.1) | copy-start | bytes 1769476
  0.9 14.2 %copy-start.5 = (s32[8]{0:T(128)S(1)}, s32[8]{0:T(128)}, u32[]{:S(2)}) copy-start(s32[8]{0:T(128)} %members_ref.1) | copy-start | bytes 100
  0.9 14.2 %copy-start.6 = (s32[8]{0:T(128)S(1)}, s32[8]{0:T(128)}, u32[]{:S(2)}) copy-start(s32[8]{0:T(128)} %lengths_ref.1) | copy-start | bytes 100
  41.7 33.4 %copy-start.11 = (bf16[2048,448]{0,1:T(8,128)(2,1)S(1)}, bf16[2048,448]{0,1:T(8,128)(2,1)}, u32[]{:S(2)}) copy-start(bf16[2048,448]{0,1:T(8,128)(2,1)} %param.19) | copy-start | bytes 5505028
  76.3 7.9 %copy-start.8 = (bf16[512,448]{0,1:T(8,128)(2,1)S(1)}, bf16[512,448]{0,1:T(8,128)(2,1)}, u32[]{:S(2)}) copy-start(bf16[512,448]{0,1:T(8,128)(2,1)} %param.17) | copy-start | bytes 1376260
  77.4 16.3 %all-to-all-start.2 = ((bf16[16,4,8,448]{3,2,0,1:T(8,128)(2,1)}), bf16[16,4,8,448]{3,2,0,1:T(8,128)(2,1)S(1)}, u32[]{:S(2)}, u32[]{:S(2)}) async-start(bf16[16,4,8,448]{3,2,0,1:T(8,128)(2,1)} %copy.44), calls=%async_computation.2 | async-start | bytes 1048576 | tf_op jit(solution)/shard_map/all_to_all | solution.py:132
  84.4 10.6 %copy-start.7 = (bf16[512,448]{1,0:T(8,128)(2,1)}, bf16[512,448]{1,0:T(8,128)(2,1)S(1)}, u32[]{:S(2)}) copy-start(bf16[512,448]{1,0:T(8,128)(2,1)S(1)} %copy.38) | copy-start | bytes 1376260
  84.4 15.7 %copy-start.9 = (bf16[448]{0:T(512)(128)(2,1)S(1)}, bf16[448]{0:T(512)(128)(2,1)}, u32[]{:S(2)}) copy-start(bf16[448]{0:T(512)(128)(2,1)} %param.20) | copy-start | bytes 2692
  95.1 18.9 %copy-start.2 = (bf16[448,2304]{1,0:T(8,128)(2,1)S(1)}, bf16[448,2304]{1,0:T(8,128)(2,1)}, u32[]{:S(2)}) copy-start(bf16[448,2304]{1,0:T(8,128)(2,1)} %gate_ref.1) | copy-start | bytes 6193156
  95.1 17.4 %all-to-all-start.3 = ((bf16[8,128,448]{1,2,0:T(8,128)(2,1)}), bf16[8,128,448]{1,2,0:T(8,128)(2,1)}, u32[]{:S(2)}, u32[]{:S(2)}) async-start(bf16[8,128,448]{1,2,0:T(8,128)(2,1)} %broadcast_in_dim.40), calls=%async_computation.3 | async-start | bytes 1835008 | tf_op jit(solution)/shard_map/all_to_all | solution.py:97
  113.9 1.6 copy-start.3
  236.1 64.4 %copy-start.10 = (bf16[2304,448]{0,1:T(8,128)(2,1)S(1)}, bf16[2304,448]{0,1:T(8,128)(2,1)}, u32[]{:S(2)}) copy-start(bf16[2304,448]{0,1:T(8,128)(2,1)} %param.23) | copy-start | bytes 6193156
  322.2 25.7 %copy-start.1 = (bf16[16,512,128]{2,1,0:T(8,128)(2,1)S(1)}, bf16[16,512,128]{2,1,0:T(8,128)(2,1)}, u32[]{:S(2)}) copy-start(bf16[16,512,128]{2,1,0:T(8,128)(2,1)} %param.18) | copy-start | bytes 6291460
